TPU v7x, 512 devices: a whole 4x8x8 slice. The times are simulated.
512 devices in a mesh: ex: 32 (over z_lo, y, core), feat: 16 (over z_hi, x).
Axes of the slice: x: 4, y: 8, z: 8 (z_hi: 4, z_lo: 2; z = z_hi * 2 + z_lo), core: 2. Of those that a mesh axis runs over, the one named last changes fastest.
Arguments:
- train_grads: bfloat16 [65536, 16384], P('ex', 'feat'), may hold values from -6 to 6
- query_grads: bfloat16 [512, 16384], P('ex', 'feat'), may hold values from -2.390625 to 2.390625
- eigenvalues: float32 [16384], P('feat'), may hold values from 0.009 to 8, as said below
Outputs:
- scores: float32 [65536, 512], P('ex', 'feat')
Inputs may be any that keep to these rules, and one draw needn't show every extreme that they name: Positive curvature eigenvalues.
All inputs are finite; a program needn't handle non-finite values.
Results may differ from a plain program's by a relative error of at most 0.0029.
Values may be sent and summed in bfloat16 or wider, within the bound.
A program may use at most 64 MiB of HBM per device.

v0:
```python
import jax
import jax.numpy as jnp
from jax import lax
from jax.sharding import PartitionSpec as P

DAMPING = 0.05
EPSILON = 1e-06


def on_device(train_grads, query_grads, eigenvalues):
    inverse = 1.0 / (eigenvalues + DAMPING)
    precond = (query_grads.astype(jnp.float32) * inverse[None, :]).astype(jnp.bfloat16)
    partial_self = jnp.sum(jnp.square(train_grads.astype(jnp.float32)) * inverse[None, :], axis=1)
    selfinf = lax.psum(partial_self, "feat")
    terms = lax.dot_general(
        train_grads,
        lax.all_gather(precond, "ex", axis=0, tiled=True),
        (((1,), (1,)), ((), ())),
        preferred_element_type=jnp.float32,
    )
    raw = lax.psum_scatter(terms, "feat", scatter_dimension=1, tiled=True)
    return raw * lax.rsqrt(selfinf + EPSILON)[:, None]


def solution(mesh):
    placed = (P("ex", "feat"), P("ex", "feat"), P("feat"))
    return jax.shard_map(
        on_device, mesh=mesh, in_specs=placed, out_specs=P("ex", "feat"), check_vma=False
    )
```

profile of v0, /device:TPU:1, one launch (start us, length us, event | category | flops | bytes accessed | tf_op | source)
XLA Modules:
  0.0 197.4 jit_solution(14690637531826796090)
XLA Ops:
  6.5 0.0 all-gather.2.cloned.1.call-start
  6.5 0.7 add_divide_fusion
  7.2 1.4 multiply_convert_fusion
  8.6 0.0 all-gather.2.cloned.1.call-update
  8.6 0.0 reduce-scatter.2.cloned.1.call-start
  8.7 73.1 %all-gather.2.cloned.1.call-done = bf16[512,1024]{1,0:T(8,128)(2,1)} async-done(((bf16[16,1024]{1,0:T(8,128)(2,1)}), bf16[512,1024]{1,0:T(8,128)(2,1)}) %all-gather.2.cloned.1.call-update) | async-done | bytes 1048592 | tf_op jit(solution)/shard_map/all_gather | solution.py:17
  81.7 6.8 %convolution_bitcast_fusion = f32[2048,512]{0,1:T(8,128)} fusion(bf16[512,1024]{1,0:T(8,128)(2,1)} %all-gather.2.cloned.1.call-done, bf16[2048,1024]{1,0:T(8,128)(2,1)} %param.3), kind=kOutput, calls=%fused_computation.1 | convolution fusion | flops 2147483648 | bytes 9437184 | tf_op jit(solution)/shard_map/dot_general | solution.py:15
  88.6 0.0 reduce-scatter.2.cloned.1.call-update
  88.6 3.3 %multiply_reduce_fusion = f32[2048]{0:T(1024)S(1)} fusion(bf16[2048,1024]{1,0:T(8,128)(2,1)} %param.3, f32[1024]{0:T(1024)S(1)} %add_divide_fusion), kind=kLoop, calls=%fused_computation | loop fusion | flops 8386560 | bytes 4206592 | tf_op jit(solution)/shard_map/reduce_sum | solution.py:13
  91.9 39.5 %psum.7 = f32[2048]{0:T(1024)S(1)} all-reduce(f32[2048]{0:T(1024)S(1)} %multiply_reduce_fusion), channel_id=1, replica_groups=mesh['ex'=32,'feat'=16] {'feat'}, use_global_device_ids=true, to_apply=%region_2.0 | all-reduce | flops 2048 | bytes 16384 | tf_op jit(solution)/shard_map/psum | solution.py:14
  131.4 57.5 %reduce-scatter.2.cloned.1.call-done = f32[2048,32]{0,1:T(8,128)} async-done(((f32[2048,512]{0,1:T(8,128)}), f32[2048,32]{0,1:T(8,128)}) %reduce-scatter.2.cloned.1.call-update) | async-done | bytes 262160 | tf_op jit(solution)/shard_map/reduce_scatter | solution.py:21
  188.9 1.7 broadcast_multiply_fusion
  (1 shorter events, 0.0 us)
Async XLA Ops:
  6.5 75.2 %all-gather.2.cloned.1.call-start = ((), (), s32[]{:S(2)}) async-start(), calls=%async_computation.1 | async-start | bytes 1081344 | tf_op jit(solution)/shard_map/all_gather | solution.py:17
  8.6 180.3 %reduce-scatter.2.cloned.1.call-start = ((), (), s32[]{:S(2)}) async-start(), calls=%async_computation.2 | async-start | bytes 4456448 | tf_op jit(solution)/shard_map/reduce_scatter | solution.py:21
Sparse Core Ops, SparseCore 0:
  9.5 72.1 all-gather.1
  88.7 100.1 reduce-scatter.1
where the time goes:
time: 198 us; the launch traced here: 197 us
  waiting for transfers between devices  131 us (66%)
  blocking collectives  39.5 us (20%)
  between operations  13.4 us (7%)
  other arithmetic  7.1 us (4%)
  matrix products  6.81 us (3%)
    all_gather x1, waiting for transfers between devices, on_device(): lax.all_gather(precond, 'ex', axis=0, tiled=True)  73.1 us
    reduce_scatter x1, waiting for transfers between devices, on_device(): raw = lax.psum_scatter(terms, 'feat', scatter_dimension=1, tiled=True)  57.5 us
    psum x1, blocking collectives, on_device(): selfinf = lax.psum(partial_self, 'feat')  39.5 us
    dot_general x1, matrix products, on_device(): lax.dot_general(train_grads, lax.all_gather(precond, 'ex', axis=0, tiled=...  6.81 us
  transfers between devices with their start and end apart: 2, of which 2 were waited for; matrix products, arithmetic and copies ran while one was open for 2% of the time, Pallas kernels for 0%

commit v1 on v0

v1 whole, which is shorter than its diff:
```python
import jax
import jax.numpy as jnp
from jax import lax
from jax.experimental import pallas as pl
from jax.experimental.pallas import tpu as pltpu
from jax.sharding import PartitionSpec as P

DAMPING = 0.05
EPSILON = 1e-06

MESH = pl.DeviceIdType.MESH
F32, BF16 = jnp.float32, jnp.bfloat16
NT = (((1,), (1,)), ((), ()))

ROWS = 2048
DEPTH = 1024
BLOCK = 16
OWNED = 32
NR = 2
R = ROWS // NR
PIECES = [(0, r) for r in range(NR)] + [(q, r) for r in range(NR) for q in (1, 2, 3)]
N = len(PIECES)
LAG = 2

OFFSETS = (0, 1, -1, 2)


def kernel(
    train_hbm, query, eig, out, train, pre, acc, xs1, xs2, xr1, xr2, zs, zr, own, sb, sr,
    load_sem, ag_send, ag_recv, x1_send, x1_recv, x2_send, x2_recv, z_send, z_recv, s_send, s_recv, far_sem,
):
    ex, feat = lax.axis_index("ex"), lax.axis_index("feat")
    core, y, z_lo = lax.rem(ex, 2), lax.rem(ex // 2, 8), ex // 16
    x, z_hi = lax.rem(feat, 4), feat // 4

    def at(dx=0, dy=0, other_z=0, other_core=0, dz=0):
        there = (lax.rem(z_lo + other_z, 2) * 8 + lax.rem(y + dy + 8, 8)) * 2 + lax.rem(core + other_core, 2)
        return {"ex": there, "feat": lax.rem(z_hi + dz + 4, 4) * 4 + lax.rem(x + dx + 4, 4)}

    barrier = pltpu.get_barrier_semaphore()
    near = [at(dx=1), at(dx=-1), at(dz=1), at(dz=-1), at(other_core=1), at(other_z=1)]
    near += [at(dy=d) for d in (1, -1, 2, -2)]
    for device in near:
        pl.semaphore_signal(barrier, inc=1, device_id=device, device_id_type=MESH)

    loads = []
    for r in range(NR):
        rows = pl.ds(r * R, R)
        load = pltpu.make_async_copy(train_hbm.at[rows], train.at[rows], load_sem.at[r])
        load.start()
        loads.append(load)

    inverse = 1.0 / (eig[...] + DAMPING)

    def slot(quad, place, sibling):
        row = lax.rem(y + OFFSETS[place] + 8, 4) * 32 + lax.rem(core + sibling, 2) * BLOCK
        return pre.at[quad, pl.ds(pl.multiple_of(row, BLOCK), BLOCK)]

    pre[0, pl.ds(pl.multiple_of(lax.rem(y, 4) * 32 + core * BLOCK, BLOCK), BLOCK), :] = (
        query[...].astype(F32) * inverse
    ).astype(BF16)

    sent = []

    def send_block(source, quad, place, sibling, device):
        index = quad * 8 + place * 2 + sibling
        row = lax.rem(y + OFFSETS[source[1]] + 8, 4) * 32 + lax.rem(core + source[2], 2) * BLOCK
        target = pre.at[quad, pl.ds(pl.multiple_of(row, BLOCK), BLOCK)]
        copy = pltpu.make_async_remote_copy(
            src_ref=slot(*source),
            dst_ref=target,
            send_sem=ag_send.at[index],
            recv_sem=ag_recv.at[index],
            device_id=device,
            device_id_type=MESH,
        )
        copy.start()
        sent.append(copy)

    def wait_block(quad, place, sibling):
        index = quad * 8 + place * 2 + sibling
        here = slot(quad, place, sibling)
        pltpu.make_async_remote_copy(
            src_ref=here,
            dst_ref=here,
            send_sem=ag_send.at[index],
            recv_sem=ag_recv.at[index],
            device_id=at(other_core=1),
            device_id_type=MESH,
        ).wait_recv()

    def forward(quad, place):
        wait_block(quad, place, 0)
        send_block((quad, place, 0), quad, place, 1, at(other_core=1))
        if quad == 0:
            send_block((0, place, 0), 1, *{1: (2, 0, at(dy=-2)), 2: (1, 0, at(dy=2)), 3: (0, 0, at(dy=-2))}[place])
        if quad < 2:
            send_block((quad, place, 0), quad + 2, place, 0, at(other_z=1))

    left, right, opposite = lax.rem(x + 3, 4), lax.rem(x + 1, 4), lax.rem(x + 2, 4)
    to_left, to_right = at(dx=-1), at(dx=1)

    def piece_rows(cls, half):
        return pl.ds(pl.multiple_of(cls * 32 + half * 16, 16), 16)

    def x_copy(which, p, side):
        source, target, send, recv = (xs1, xr1, x1_send, x1_recv) if which == 1 else (xs2, xr2, x2_send, x2_recv)
        return pltpu.make_async_remote_copy(
            src_ref=source.at[p, side],
            dst_ref=target.at[p, side],
            send_sem=send.at[p, side],
            recv_sem=recv.at[p, side],
            device_id=(to_left, to_right)[side],
            device_id_type=MESH,
        )

    def multiply(p):
        quad, r = PIECES[p]
        acc[p] = lax.dot_general(pre[quad], train[pl.ds(r * R, R), :], NT, preferred_element_type=F32)
        xs1[p, 0, 0:16] = acc[p, piece_rows(opposite, 0), :].astype(BF16)
        xs1[p, 0, 16:32] = acc[p, piece_rows(left, 1), :].astype(BF16)
        x_copy(1, p, 0).start()
        xs1[p, 1, 0:16] = acc[p, piece_rows(right, 0), :].astype(BF16)
        xs1[p, 1, 16:32] = acc[p, piece_rows(opposite, 1), :].astype(BF16)
        x_copy(1, p, 1).start()

    def relay(p):
        x_copy(1, p, 0).wait_recv()
        xs2[p, 0] = (acc[p, piece_rows(left, 0), :] + xr1[p, 0, 0:16].astype(F32)).astype(BF16)
        x_copy(2, p, 0).start()
        x_copy(1, p, 1).wait_recv()
        xs2[p, 1] = (acc[p, piece_rows(right, 1), :] + xr1[p, 1, 16:32].astype(F32)).astype(BF16)
        x_copy(2, p, 1).start()

    away = lax.rem(x - y + 9, 4) - 1
    bit = lax.rem(y + away + 8, 8) // 4

    def steps_to_owner(quad):
        owner = lax.rem(z_lo + quad // 2, 2) * 2 + lax.rem(bit + quad % 2, 2)
        return lax.rem(z_hi - owner + 4, 4)

    def z_copy(steps, p, r):
        return pltpu.make_async_remote_copy(
            src_ref=zs.at[p],
            dst_ref=zr.at[steps - 1, r],
            send_sem=z_send.at[steps - 1, r],
            recv_sem=z_recv.at[steps - 1, r],
            device_id=at(dz=-steps),
            device_id_type=MESH,
        )

    def collect(p):
        quad, r = PIECES[p]
        x_copy(2, p, 0).wait_recv()
        x_copy(2, p, 1).wait_recv()
        upper = acc[p, piece_rows(x, 0), :] + (xr2[p, 0].astype(F32) + xr1[p, 1, 0:16].astype(F32))
        lower = acc[p, piece_rows(x, 1), :] + (xr1[p, 0, 16:32].astype(F32) + xr2[p, 1].astype(F32))
        steps = steps_to_owner(quad)

        @pl.when(steps == 0)
        def _():
            own[r, 0:16] = upper
            own[r, 16:32] = lower

        @pl.when(steps != 0)
        def _():
            zs[p, 0:16] = upper.astype(BF16)
            zs[p, 16:32] = lower.astype(BF16)
            z_copy(steps, p, r).start()

    def other_x(first):
        there = x + 1 - 2 * lax.rem(x, 2) if first else 3 - x
        return {"ex": ex, "feat": z_hi * 4 + there}

    def other_z_hi(first):
        there = z_hi + 1 - 2 * lax.rem(z_hi, 2) if first else 3 - z_hi
        return {"ex": ex, "feat": there * 4 + x}

    partners = [other_x(True), other_x(False), other_z_hi(True), other_z_hi(False)]

    def self_copy(step):
        return pltpu.make_async_remote_copy(
            src_ref=sb.at[step],
            dst_ref=sr.at[step],
            send_sem=s_send.at[step],
            recv_sem=s_recv.at[step],
            device_id=partners[step],
            device_id_type=MESH,
        )

    def self_step(step):
        self_copy(step).wait_recv()
        sb[step + 1] = sb[step] + sr[step]
        if step < 3:
            self_copy(step + 1).start()

    pl.semaphore_wait(barrier, len(near))
    send_block((0, 0, 0), 0, 1, 0, at(dy=-1))
    send_block((0, 0, 0), 0, 2, 0, at(dy=1))
    send_block((0, 0, 0), 0, 3, 0, at(dy=-2))
    send_block((0, 0, 0), 0, 0, 1, at(other_core=1))
    send_block((0, 0, 0), 1, 3, 0, at(dy=2))
    send_block((0, 0, 0), 2, 0, 0, at(other_z=1))
    pl.semaphore_signal(far_sem, inc=1, device_id=at(dz=1), device_id_type=MESH)

    ones = jnp.ones((8, 128), F32)
    for r in range(NR):
        loads[r].wait()
        wide = train[pl.ds(r * R, R), :].astype(F32)
        squares = wide * wide * inverse
        part = squares[:, 0:128]
        for k in range(1, DEPTH // 128):
            part = part + squares[:, k * 128 : (k + 1) * 128]
        sums = lax.dot_general(ones, part, NT, preferred_element_type=F32, precision=lax.Precision.HIGHEST)
        for k in range(8 // NR):
            sb[0, pl.ds(r * (8 // NR) + k, 1), :] = sums[0:1, k * 256 : (k + 1) * 256]
    self_copy(0).start()

    forward(0, 1)
    forward(0, 2)
    forward(0, 3)
    for place in range(4):
        wait_block(0, place, 1)

    for t in range(N + 2 * LAG):
        if t < N:
            if t == NR:
                for place in (3, 2, 1, 0):
                    forward(1, place)
                for place in range(4):
                    wait_block(1, place, 1)
            elif t == NR + 1:
                for place in range(4):
                    wait_block(2, place, 1)
                for place in (3, 2, 1, 0):
                    forward(3, place)
            elif t == NR + 2:
                for place in range(4):
                    wait_block(3, place, 1)
            multiply(t)
        if t == NR - 1:
            for place in range(4):
                forward(2, place)
        if t == 2 * LAG:
            pl.semaphore_wait(far_sem, 1)
        if 0 <= t - LAG < N:
            relay(t - LAG)
        if 2 <= t < 6:
            self_step(t - 2)
        if t >= 2 * LAG:
            collect(t - 2 * LAG)

    scale = lax.rsqrt(sb[4] + EPSILON)
    for r in range(NR):
        for steps in (1, 2, 3):
            z_copy(steps, 0, r).wait_recv()
        total = own[r] + zr[0, r].astype(F32) + zr[1, r].astype(F32) + zr[2, r].astype(F32)
        for k in range(8 // NR):
            i = r * (8 // NR) + k
            out[:, i * 256 : (i + 1) * 256] = total[:, k * 256 : (k + 1) * 256] * scale[i : i + 1, :]

    for copy in sent:
        copy.wait_send()
    for p in range(N):
        for side in (0, 1):
            x_copy(1, p, side).wait_send()
            x_copy(2, p, side).wait_send()
    for r in range(NR):
        for steps in (1, 2, 3):
            z_copy(steps, 0, r).wait_send()
    for step in range(4):
        self_copy(step).wait_send()


def on_device(train_grads, query_grads, eigenvalues):
    dma = pltpu.SemaphoreType.DMA
    scores = pl.pallas_call(
        kernel,
        out_shape=jax.ShapeDtypeStruct((OWNED, ROWS), F32),
        in_specs=[
            pl.BlockSpec(memory_space=pl.ANY),
            pl.BlockSpec(memory_space=pltpu.VMEM),
            pl.BlockSpec(memory_space=pltpu.VMEM),
        ],
        out_specs=pl.BlockSpec(memory_space=pltpu.VMEM),
        scratch_shapes=[
            pltpu.VMEM((ROWS, DEPTH), BF16),
            pltpu.VMEM((4, 128, DEPTH), BF16),
            pltpu.VMEM((N, 128, R), F32),
            pltpu.VMEM((N, 2, 32, R), BF16),
            pltpu.VMEM((N, 2, 16, R), BF16),
            pltpu.VMEM((N, 2, 32, R), BF16),
            pltpu.VMEM((N, 2, 16, R), BF16),
            pltpu.VMEM((N, OWNED, R), BF16),
            pltpu.VMEM((3, NR, OWNED, R), BF16),
            pltpu.VMEM((NR, OWNED, R), F32),
            pltpu.VMEM((5, 8, 256), F32),
            pltpu.VMEM((4, 8, 256), F32),
            dma((NR,)),
            dma((32,)),
            dma((32,)),
            dma((N, 2)),
            dma((N, 2)),
            dma((N, 2)),
            dma((N, 2)),
            dma((3, NR)),
            dma((3, NR)),
            dma((4,)),
            dma((4,)),
            pltpu.SemaphoreType.REGULAR,
        ],
        compiler_params=pltpu.CompilerParams(
            collective_id=0, has_side_effects=True, vmem_limit_bytes=48 * 2**20
        ),
        cost_estimate=pl.CostEstimate(flops=2 * ROWS * DEPTH * 512, bytes_accessed=6 * 2**20, transcendentals=0),
    )(train_grads, query_grads, eigenvalues.reshape(1, DEPTH))
    return scores.T


def solution(mesh):
    placed = (P("ex", "feat"), P("ex", "feat"), P("feat"))
    return jax.shard_map(
        on_device, mesh=mesh, in_specs=placed, out_specs=P("ex", "feat"), check_vma=False
    )
```

time: 198 us -> 54.9 us (0.28)
  the two profiles are of different devices: /device:TPU:1 before, /device:TPU:70 now
where the time goes in v1:
time: 54.9 us; the launch traced here: 54.6 us
  Pallas kernels  50.3 us (92%)
  local copies, waits for them, and re-layouts  4.34 us (8%)
    pallas_call x1, Pallas kernels, on_device(): pl.pallas_call(kernel, out_shape=jax.ShapeDtypeStruct((OWNED, ROWS), F32)...  50.3 us
    unnamed x7, local copies, waits for them, and re-layouts  4.34 us

profile of v1, /device:TPU:70, one launch (start us, length us, event | category | flops | bytes accessed | tf_op | source)
XLA Modules:
  0.0 54.6 jit_solution(13083773668928985974)
XLA Ops:
  0.0 0.0 copy-start
  0.0 2.2 %copy-done = bf16[2048,1024]{1,0:T(8,128)(2,1)S(1)} copy-done((bf16[2048,1024]{1,0:T(8,128)(2,1)S(1)}, bf16[2048,1024]{1,0:T(8,128)(2,1)}, u32[]{:S(2)}) %copy-start) | copy-done | bytes 4194328
  2.2 0.0 copy-start.1
  2.2 0.8 %copy-done.1 = bf16[16,1024]{1,0:T(8,128)(2,1)S(1)} copy-done((bf16[16,1024]{1,0:T(8,128)(2,1)S(1)}, bf16[16,1024]{1,0:T(8,128)(2,1)}, u32[]{:S(2)}) %copy-start.1) | copy-done | bytes 32792
  2.9 0.0 copy-start.2
  2.9 0.7 %copy-done.2 = f32[1024]{0:T(1024)S(1)} copy-done((f32[1024]{0:T(1024)S(1)}, f32[1024]{0:T(1024)}, u32[]{:S(2)}) %copy-start.2) | copy-done | bytes 4120
  3.6 50.3 %shard_map.37 = f32[32,2048]{1,0:T(8,128)S(1)} custom-call(bf16[2048,1024]{1,0:T(8,128)(2,1)S(1)} %copy-done, bf16[16,1024]{1,0:T(8,128)(2,1)S(1)} %copy-done.1, f32[1,1024]{1,0:T(1,128)S(1)} %bitcast.3), custom_call_target="tpu_custom_call" | custom-call | flops 2147483648 | bytes 6291456 | tf_op jit(solution)/shard_map/pallas_call | solution.py:277
  53.9 0.7 %copy.5 = f32[2048,32]{0,1:T(8,128)} copy(f32[2048,32]{0,1:T(8,128)S(1)} %bitcast.2) | data formatting | bytes 524288
Async XLA Ops:
  0.0 2.2 %copy-start = (bf16[2048,1024]{1,0:T(8,128)(2,1)S(1)}, bf16[2048,1024]{1,0:T(8,128)(2,1)}, u32[]{:S(2)}) copy-start(bf16[2048,1024]{1,0:T(8,128)(2,1)} %train_hbm.1) | copy-start | bytes 12582916
  2.2 0.8 %copy-start.1 = (bf16[16,1024]{1,0:T(8,128)(2,1)S(1)}, bf16[16,1024]{1,0:T(8,128)(2,1)}, u32[]{:S(2)}) copy-start(bf16[16,1024]{1,0:T(8,128)(2,1)} %query.1) | copy-start | bytes 98308
  2.9 0.7 %copy-start.2 = (f32[1024]{0:T(1024)S(1)}, f32[1024]{0:T(1024)}, u32[]{:S(2)}) copy-start(f32[1024]{0:T(1024)} %param.5) | copy-start | bytes 12292

commit v2 on v0

v2 whole, which is shorter than its diff:
```python
import jax
import jax.numpy as jnp
from jax import lax
from jax.experimental import pallas as pl
from jax.experimental.pallas import tpu as pltpu
from jax.sharding import PartitionSpec as P

DAMPING = 0.05
EPSILON = 1e-06

MESH = pl.DeviceIdType.MESH
F32, BF16 = jnp.float32, jnp.bfloat16
NT = (((1,), (1,)), ((), ()))

ROWS = 2048
DEPTH = 1024
BLOCK = 16
OWNED = 32

OFFSETS = (0, 1, -1, 2)
RUNS = ((0, 512), (512, 1024), (1536, 512))
RELAYED = 1
LONG = RUNS[RELAYED][1]
STRAIGHT = {0: (0, 0), 2: (1, 512)}


def kernel(
    train_hbm, query_hbm, eig_hbm, out, train, query, eig, pre, keep, xs, xr, zs, zr, zkeep, ds, dr, own, sb, sr,
    load_sem, ag_send, ag_recv, x_send, x_recv, z_send, z_recv, d_send, d_recv, s_send, s_recv,
):
    ex, feat = lax.axis_index("ex"), lax.axis_index("feat")
    core, y, z_lo = lax.rem(ex, 2), lax.rem(ex // 2, 8), ex // 16
    x, z_hi = lax.rem(feat, 4), feat // 4

    def at(dx=0, dy=0, other_z=0, other_core=0, dz=0):
        there = (lax.rem(z_lo + other_z, 2) * 8 + lax.rem(y + dy + 8, 8)) * 2 + lax.rem(core + other_core, 2)
        return {"ex": there, "feat": lax.rem(z_hi + dz + 4, 4) * 4 + lax.rem(x + dx + 4, 4)}

    barrier = pltpu.get_barrier_semaphore()
    near = [at(other_core=1), at(other_z=1)] + [at(dy=d) for d in (1, -1, 2, -2)]
    near += [at(dx=1), at(dx=-1)] + [at(dz=d) for d in (1, -1, 2)]
    for device in near:
        pl.semaphore_signal(barrier, inc=1, device_id=device, device_id_type=MESH)

    small = [
        pltpu.make_async_copy(query_hbm, query, load_sem.at[len(RUNS)]),
        pltpu.make_async_copy(eig_hbm, eig, load_sem.at[len(RUNS) + 1]),
    ]
    for load in small:
        load.start()
    loads = []
    for r, run in enumerate(RUNS):
        rows = pl.ds(*run)
        load = pltpu.make_async_copy(train_hbm.at[rows], train.at[rows], load_sem.at[r])
        load.start()
        loads.append(load)
    for load in small:
        load.wait()
    inverse = 1.0 / (eig[...] + DAMPING)

    def slot(quad, place, block_place, sibling):
        role = lax.rem(y + OFFSETS[block_place] - x + 8, 4)
        half = lax.rem(core + sibling, 2) * BLOCK
        return pre.at[quad, pl.ds(pl.multiple_of(role * 32 + half, BLOCK), BLOCK)]

    def block_copy(source, target, device):
        quad, place, sibling = target
        index = quad * 8 + place * 2 + sibling
        return pltpu.make_async_remote_copy(
            src_ref=slot(source[0], source[1], source[1], source[2]),
            dst_ref=slot(quad, place, source[1], source[2]),
            send_sem=ag_send.at[index],
            recv_sem=ag_recv.at[index],
            device_id=device,
            device_id_type=MESH,
        )

    sent = []

    def send_block(source, target, device):
        copy = block_copy(source, target, device)
        copy.start()
        sent.append(copy)

    def wait_block(quad, place, sibling):
        block_copy((quad, place, sibling), (quad, place, sibling), at(other_core=1)).wait_recv()

    beyond = {1: (2, -2), 2: (1, 2), 3: (0, -2)}

    def forward(quad, place):
        wait_block(quad, place, 0)
        here = (quad, place, 0)
        send_block(here, (quad, place, 1), at(other_core=1))
        if quad < 2:
            send_block(here, (quad + 2, place, 0), at(other_z=1))
        if quad == 0:
            further, step = beyond[place]
            send_block(here, (1, further, 0), at(dy=step))

    to_left, to_right = at(dx=-1), at(dx=1)

    def x_copy(quad, r, side, kind):
        rows = pl.ds(*RUNS[r])
        piece = quad * len(RUNS) + r
        return pltpu.make_async_remote_copy(
            src_ref=xs.at[quad, side, kind, :, rows],
            dst_ref=xr.at[quad, side, kind, :, rows],
            send_sem=x_send.at[piece, side, kind],
            recv_sem=x_recv.at[piece, side, kind],
            device_id=(to_left, to_right)[side],
            device_id_type=MESH,
        )

    def multiply(quad, r):
        rows = pl.ds(*RUNS[r])
        product = lax.dot_general(pre[quad], train[rows, :], NT, preferred_element_type=F32)
        xs[quad, 0, 0, :, rows] = product[64:80].astype(BF16)
        xs[quad, 1, 0, :, rows] = product[80:96].astype(BF16)
        x_copy(quad, r, 0, 0).start()
        x_copy(quad, r, 1, 0).start()
        xs[quad, 0, 1, :, rows] = product[112:128].astype(BF16)
        xs[quad, 1, 1, :, rows] = product[32:48].astype(BF16)
        x_copy(quad, r, 0, 1).start()
        x_copy(quad, r, 1, 1).start()
        keep[quad, 0:32, rows] = product[0:32]
        keep[quad, 32:48, rows] = product[96:112]
        keep[quad, 48:64, rows] = product[48:64]

    def relay(quad, r):
        rows = pl.ds(*RUNS[r])
        for side in (0, 1):
            x_copy(quad, r, side, 0).wait_recv()
            mine = keep[quad, 32 + side * 16 : 48 + side * 16, rows]
            xs[quad, side, 2, :, rows] = (mine + xr[quad, side, 0, :, rows].astype(F32)).astype(BF16)
            x_copy(quad, r, side, 2).start()

    bit = lax.rem(y + lax.rem(x - y + 9, 4) - 1 + 8, 8) // 4

    def steps_to_owner(quad):
        owner = lax.rem(z_lo + quad // 2, 2) * 2 + lax.rem(bit + quad % 2, 2)
        return lax.rem(z_hi - owner + 4, 4)

    to_down, to_up = at(dz=-1), at(dz=1)

    def z_copy(kind):
        return pltpu.make_async_remote_copy(
            src_ref=zs.at[kind],
            dst_ref=zr.at[kind],
            send_sem=z_send.at[kind],
            recv_sem=z_recv.at[kind],
            device_id=(to_down, to_up)[kind % 2],
            device_id_type=MESH,
        )

    def direct_copy(steps, r):
        i, start = STRAIGHT[r]
        rows = pl.ds(start, RUNS[r][1])
        return pltpu.make_async_remote_copy(
            src_ref=ds.at[steps - 1, :, rows],
            dst_ref=dr.at[steps - 1, :, rows],
            send_sem=d_send.at[steps - 1, i],
            recv_sem=d_recv.at[steps - 1, i],
            device_id=at(dz=-steps),
            device_id_type=MESH,
        )

    def collect(quad, r):
        start, count = RUNS[r]
        rows = pl.ds(start, count)
        for side in (0, 1):
            x_copy(quad, r, side, 1).wait_recv()
            x_copy(quad, r, side, 2).wait_recv()
        got = lambda side, kind: xr[quad, side, kind, :, rows].astype(F32)
        upper = keep[quad, 0:16, rows] + (got(0, 2) + got(1, 1))
        lower = keep[quad, 16:32, rows] + (got(0, 1) + got(1, 2))
        steps = steps_to_owner(quad)

        @pl.when(steps == 0)
        def _():
            own[0:16, rows] = upper
            own[16:32, rows] = lower

        if r != RELAYED:

            @pl.when(steps != 0)
            def _():
                ds[steps - 1, 0:16, pl.ds(STRAIGHT[r][1], count)] = upper.astype(BF16)
                ds[steps - 1, 16:32, pl.ds(STRAIGHT[r][1], count)] = lower.astype(BF16)
                direct_copy(steps, r).start()

            return

        @pl.when(steps == 2)
        def _():
            zs[0] = upper.astype(BF16)
            zs[1] = lower.astype(BF16)
            z_copy(0).start()
            z_copy(1).start()

        @pl.when(steps == 1)
        def _():
            zs[2] = lower.astype(BF16)
            z_copy(2).start()
            zkeep[0] = upper

        @pl.when(steps == 3)
        def _():
            zs[3] = upper.astype(BF16)
            z_copy(3).start()
            zkeep[1] = lower

    def z_relay():
        for side in (0, 1):
            z_copy(side).wait_recv()
            zs[4 + side] = (zkeep[side] + zr[side].astype(F32)).astype(BF16)
            z_copy(4 + side).start()

    def finish(r, scale):
        start, count = RUNS[r]
        rows = pl.ds(start, count)
        if r == RELAYED:
            for kind in (2, 3, 4, 5):
                z_copy(kind).wait_recv()
            upper = own[0:16, rows] + (zr[4].astype(F32) + zr[3].astype(F32))
            lower = own[16:32, rows] + (zr[2].astype(F32) + zr[5].astype(F32))
        else:
            for steps in (1, 2, 3):
                direct_copy(steps, r).wait_recv()
            parts = dr[:, :, pl.ds(STRAIGHT[r][1], count)].astype(F32)
            total = own[:, rows] + (parts[0] + parts[1] + parts[2])
            upper, lower = total[0:16], total[16:32]
        for k in range(count // 256):
            i = start // 256 + k
            columns = slice(k * 256, (k + 1) * 256)
            out[0:16, i * 256 : (i + 1) * 256] = upper[:, columns] * scale[i : i + 1, :]
            out[16:32, i * 256 : (i + 1) * 256] = lower[:, columns] * scale[i : i + 1, :]

    def partner(step):
        pair = lambda i: i + 1 - 2 * lax.rem(i, 2)
        if step < 2:
            return {"ex": ex, "feat": z_hi * 4 + (pair(x) if step == 0 else 3 - x)}
        return {"ex": ex, "feat": (pair(z_hi) if step == 2 else 3 - z_hi) * 4 + x}

    def self_copy(step):
        return pltpu.make_async_remote_copy(
            src_ref=sb.at[step],
            dst_ref=sr.at[step],
            send_sem=s_send.at[step],
            recv_sem=s_recv.at[step],
            device_id=partner(step),
            device_id_type=MESH,
        )

    def self_step(step):
        self_copy(step).wait_recv()
        sb[step + 1] = sb[step] + sr[step]
        if step < 3:
            self_copy(step + 1).start()

    mine = lax.rem(y - x + 8, 4) * 32 + core * BLOCK
    pre[0, pl.ds(pl.multiple_of(mine, BLOCK), BLOCK), :] = (query[...].astype(F32) * inverse).astype(BF16)

    ones = jnp.ones((8, 128), F32)

    def self_influence(r):
        start, count = RUNS[r]
        loads[r].wait()
        wide = train[pl.ds(start, count), :].astype(F32)
        squares = wide * wide * inverse
        part = squares[:, 0:128]
        for k in range(1, DEPTH // 128):
            part = part + squares[:, k * 128 : (k + 1) * 128]
        sums = lax.dot_general(ones, part, NT, preferred_element_type=F32, precision=lax.Precision.HIGHEST)
        for k in range(count // 256):
            sb[0, pl.ds(start // 256 + k, 1), :] = sums[0:1, k * 256 : (k + 1) * 256]

    pl.semaphore_wait(barrier, len(near))
    here = (0, 0, 0)
    send_block(here, (0, 1, 0), at(dy=-1))
    send_block(here, (0, 2, 0), at(dy=1))
    send_block(here, (0, 3, 0), at(dy=-2))
    send_block(here, (0, 0, 1), at(other_core=1))
    send_block(here, (2, 0, 0), at(other_z=1))
    send_block(here, (1, 3, 0), at(dy=2))
    for r in range(len(RUNS)):
        self_influence(r)
    self_copy(0).start()

    for place in (1, 2, 3):
        forward(0, place)
    for place in (0, 1, 2, 3):
        wait_block(0, place, 1)
    multiply(0, 0)
    forward(2, 0)
    multiply(0, 1)
    forward(1, 3)
    multiply(0, 2)
    for place in (1, 2, 3):
        forward(2, place)
    self_step(0)
    for place in (0, 1, 2, 3):
        wait_block(2, place, 1)
    multiply(2, 0)
    for place in (2, 1, 0):
        forward(1, place)
    relay(0, 0)
    multiply(2, 1)
    relay(0, 1)
    multiply(2, 2)
    relay(0, 2)
    for place in (0, 1, 2, 3):
        wait_block(1, place, 1)
    multiply(1, 0)
    self_step(1)
    relay(2, 0)
    for place in (3, 2, 1, 0):
        forward(3, place)
    collect(0, 0)
    relay(2, 1)
    relay(2, 2)
    for place in (0, 1, 2, 3):
        wait_block(3, place, 1)
    multiply(3, 0)
    multiply(1, 1)
    collect(0, 1)
    collect(0, 2)
    relay(1, 0)
    multiply(3, 1)
    multiply(1, 2)
    multiply(3, 2)
    collect(2, 0)
    relay(3, 0)
    relay(1, 1)
    self_step(2)
    collect(2, 1)
    collect(2, 2)
    relay(3, 1)
    collect(1, 0)
    relay(1, 2)
    relay(3, 2)
    collect(3, 0)
    self_step(3)
    scale = lax.rsqrt(sb[4] + EPSILON)
    collect(1, 1)
    collect(3, 1)
    collect(1, 2)
    collect(3, 2)
    z_relay()
    finish(0, scale)
    finish(1, scale)
    finish(2, scale)

    for copy in sent:
        copy.wait_send()
    for quad in range(4):
        for r in range(len(RUNS)):
            for side in (0, 1):
                for kind in range(3):
                    x_copy(quad, r, side, kind).wait_send()
    for kind in range(6):
        z_copy(kind).wait_send()
    for steps in (1, 2, 3):
        for r in STRAIGHT:
            direct_copy(steps, r).wait_send()
    for step in range(4):
        self_copy(step).wait_send()


def on_device(train_grads, query_grads, eigenvalues):
    dma = pltpu.SemaphoreType.DMA
    scores = pl.pallas_call(
        kernel,
        out_shape=pltpu.VMEM((OWNED, ROWS), F32),
        in_specs=[pl.BlockSpec(memory_space=pltpu.HBM)] * 3,
        out_specs=pl.BlockSpec(memory_space=pltpu.VMEM),
        scratch_shapes=[
            pltpu.VMEM((ROWS, DEPTH), BF16),
            pltpu.VMEM((BLOCK, DEPTH), BF16),
            pltpu.VMEM((1, DEPTH), F32),
            pltpu.VMEM((4, 128, DEPTH), BF16),
            pltpu.VMEM((4, 64, ROWS), F32),
            pltpu.VMEM((4, 2, 3, 16, ROWS), BF16),
            pltpu.VMEM((4, 2, 3, 16, ROWS), BF16),
            pltpu.VMEM((6, 16, LONG), BF16),
            pltpu.VMEM((6, 16, LONG), BF16),
            pltpu.VMEM((2, 16, LONG), F32),
            pltpu.VMEM((3, OWNED, ROWS - LONG), BF16),
            pltpu.VMEM((3, OWNED, ROWS - LONG), BF16),
            pltpu.VMEM((OWNED, ROWS), F32),
            pltpu.VMEM((5, 8, 256), F32),
            pltpu.VMEM((4, 8, 256), F32),
            dma((len(RUNS) + 2,)),
            dma((32,)),
            dma((32,)),
            dma((4 * len(RUNS), 2, 3)),
            dma((4 * len(RUNS), 2, 3)),
            dma((6,)),
            dma((6,)),
            dma((3, len(STRAIGHT))),
            dma((3, len(STRAIGHT))),
            dma((4,)),
            dma((4,)),
        ],
        compiler_params=pltpu.CompilerParams(
            collective_id=0, has_side_effects=True, vmem_limit_bytes=60 * 2**20
        ),
        cost_estimate=pl.CostEstimate(flops=2 * ROWS * DEPTH * 512, bytes_accessed=6 * 2**20, transcendentals=0),
    )(train_grads, query_grads, eigenvalues.reshape(1, DEPTH))
    return scores.T


def solution(mesh):
    placed = (P("ex", "feat"), P("ex", "feat"), P("feat"))
    return jax.shard_map(
        on_device, mesh=mesh, in_specs=placed, out_specs=P("ex", "feat"), check_vma=False
    )
```

time: 198 us -> 50.2 us (0.25)
  the two profiles are of different devices: /device:TPU:1 before, /device:TPU:16 now
where the time goes in v2:
time: 50.2 us; the launch traced here: 50.1 us
  Pallas kernels  49.4 us (98%)
  local copies, waits for them, and re-layouts  0.71 us (1%)
    pallas_call x1, Pallas kernels, on_device(): pl.pallas_call(kernel, out_shape=pltpu.VMEM((OWNED, ROWS), F32), in_specs...  49.4 us

profile of v2, /device:TPU:16, one launch (start us, length us, event | category | flops | bytes accessed | tf_op | source)
XLA Modules:
  0.0 50.1 jit_solution(9967882757811372098)
XLA Ops:
  0.0 49.4 %shard_map.37 = f32[32,2048]{1,0:T(8,128)S(1)} custom-call(bf16[2048,1024]{1,0:T(8,128)(2,1)} %train_hbm.1, bf16[16,1024]{1,0:T(8,128)(2,1)} %query_hbm.1, f32[1,1024]{1,0:T(1,128)} %bitcast.3), custom_call_target="tpu_custom_call" | custom-call | flops 2147483648 | bytes 6291456 | tf_op jit(solution)/shard_map/pallas_call | solution.py:371
  49.4 0.7 %copy.5 = f32[2048,32]{0,1:T(8,128)} copy(f32[2048,32]{0,1:T(8,128)S(1)} %bitcast.2) | data formatting | bytes 524288

commit v3 on v2

--- a/solution.py
+++ b/solution.py
@@ -18,10 +18,10 @@
 OWNED = 32
 
 OFFSETS = (0, 1, -1, 2)
-RUNS = ((0, 512), (512, 1024), (1536, 512))
+RUNS = ((0, 768), (768, 768), (1536, 512))
 RELAYED = 1
 LONG = RUNS[RELAYED][1]
-STRAIGHT = {0: (0, 0), 2: (1, 512)}
+STRAIGHT = {0: (0, 0), 2: (1, 768)}
 
 
 def kernel(
@@ -85,17 +85,17 @@
     def wait_block(quad, place, sibling):
         block_copy((quad, place, sibling), (quad, place, sibling), at(other_core=1)).wait_recv()
 
-    beyond = {1: (2, -2), 2: (1, 2), 3: (0, -2)}
+    beyond = {0: (3, 2), 1: (2, -2), 2: (1, 2), 3: (0, -2)}
 
     def forward(quad, place):
         wait_block(quad, place, 0)
         here = (quad, place, 0)
         send_block(here, (quad, place, 1), at(other_core=1))
-        if quad < 2:
+        if quad == 0:
             send_block(here, (quad + 2, place, 0), at(other_z=1))
-        if quad == 0:
+        if quad in (0, 2):
             further, step = beyond[place]
-            send_block(here, (1, further, 0), at(dy=step))
+            send_block(here, (quad + 1, further, 0), at(dy=step))
 
     to_left, to_right = at(dx=-1), at(dx=1)
 
@@ -120,14 +120,41 @@
         x_copy(quad, r, 1, 0).start()
         xs[quad, 0, 1, :, rows] = product[112:128].astype(BF16)
         xs[quad, 1, 1, :, rows] = product[32:48].astype(BF16)
-        x_copy(quad, r, 0, 1).start()
-        x_copy(quad, r, 1, 1).start()
+        if not (quad != 0):
+            x_copy(quad, r, 0, 1).start()
+            x_copy(quad, r, 1, 1).start()
         keep[quad, 0:32, rows] = product[0:32]
         keep[quad, 32:48, rows] = product[96:112]
         keep[quad, 48:64, rows] = product[48:64]
 
+    def multiply_half(other):
+        half = lax.rem(core + other, 2)
+        rows = pl.ds(*RUNS[0])
+        roles = (0, 2, 1 + 2 * half, 3 - 2 * half)
+        queries = [pre[0, pl.ds(pl.multiple_of(role * 32 + half * 16, 16), 16), :] for role in roles]
+        product = lax.dot_general(jnp.concatenate(queries), train[rows, :], NT, preferred_element_type=F32)
+
+        def send(side, kind, value):
+            xs[0, side, kind, :, rows] = value.astype(BF16)
+            pltpu.make_async_remote_copy(
+                src_ref=xs.at[0, side, kind, :, rows],
+                dst_ref=xr.at[0, side, kind, :, rows],
+                send_sem=x_send.at[0, side, kind],
+                recv_sem=x_recv.at[0, side, kind],
+                device_id=at(dx=2 * side - 1),
+                device_id_type=MESH,
+            ).start()
+
+        send(half, 0, product[16:32])
+        send(1 - half, 1, product[32:48])
+        keep[0, pl.ds(pl.multiple_of(half * 16, 16), 16), rows] = product[0:16]
+        keep[0, pl.ds(pl.multiple_of(32 + half * 16, 16), 16), rows] = product[48:64]
+
     def relay(quad, r):
         rows = pl.ds(*RUNS[r])
+        if quad != 0:
+            x_copy(quad, r, 0, 1).start()
+            x_copy(quad, r, 1, 1).start()
         for side in (0, 1):
             x_copy(quad, r, side, 0).wait_recv()
             mine = keep[quad, 32 + side * 16 : 48 + side * 16, rows]
@@ -280,17 +307,19 @@
     send_block(here, (0, 2, 0), at(dy=1))
     send_block(here, (0, 3, 0), at(dy=-2))
     send_block(here, (0, 0, 1), at(other_core=1))
+    self_influence(0)
     send_block(here, (2, 0, 0), at(other_z=1))
     send_block(here, (1, 3, 0), at(dy=2))
-    for r in range(len(RUNS)):
-        self_influence(r)
+    self_influence(1)
+    self_influence(2)
     self_copy(0).start()
 
     for place in (1, 2, 3):
         forward(0, place)
+    multiply_half(0)
     for place in (0, 1, 2, 3):
         wait_block(0, place, 1)
-    multiply(0, 0)
+    multiply_half(1)
     forward(2, 0)
     multiply(0, 1)
     forward(1, 3)

time: 50.2 us -> 49.7 us (0.990)
    pallas_call x1, Pallas kernels: 49.4 us -> 48.9 us  [on_device(): pl.pallas_call(kernel, out_shape=pltpu.VMEM((OWNED, ROWS), F32), in_specs...]
where the time goes in v3:
time: 49.7 us; the launch traced here: 49.6 us
  Pallas kernels  48.9 us (98%)
  local copies, waits for them, and re-layouts  0.71 us (1%)
    pallas_call x1, Pallas kernels, on_device(): pl.pallas_call(kernel, out_shape=pltpu.VMEM((OWNED, ROWS), F32), in_specs...  48.9 us

profile of v3, /device:TPU:16, one launch (start us, length us, event | category | flops | bytes accessed | tf_op | source)
XLA Modules:
  0.0 49.6 jit_solution(4887753565173333255)
XLA Ops:
  0.0 48.9 %shard_map.37 = f32[32,2048]{1,0:T(8,128)S(1)} custom-call(bf16[2048,1024]{1,0:T(8,128)(2,1)} %train_hbm.1, bf16[16,1024]{1,0:T(8,128)(2,1)} %query_hbm.1, f32[1,1024]{1,0:T(1,128)} %bitcast.3), custom_call_target="tpu_custom_call" | custom-call | flops 2147483648 | bytes 6291456 | tf_op jit(solution)/shard_map/pallas_call | solution.py:400
  48.9 0.7 %copy.5 = f32[2048,32]{0,1:T(8,128)} copy(f32[2048,32]{0,1:T(8,128)S(1)} %bitcast.2) | data formatting | bytes 524288

commit v4 on v3

--- a/solution.py
+++ b/solution.py
@@ -336,10 +336,10 @@
     multiply(2, 1)
     relay(0, 1)
     multiply(2, 2)
-    relay(0, 2)
     for place in (0, 1, 2, 3):
         wait_block(1, place, 1)
     multiply(1, 0)
+    relay(0, 2)
     self_step(1)
     relay(2, 0)
     for place in (3, 2, 1, 0):

time: 49.7 us -> 49.7 us (level)
  no operation moved by 1% of the time
where the time goes in v4:
time: 49.7 us; the launch traced here: 49.6 us
  Pallas kernels  48.9 us (98%)
  local copies, waits for them, and re-layouts  0.71 us (1%)
    pallas_call x1, Pallas kernels, on_device(): pl.pallas_call(kernel, out_shape=pltpu.VMEM((OWNED, ROWS), F32), in_specs...  48.9 us

profile of v4, /device:TPU:16, one launch (start us, length us, event | category | flops | bytes accessed | tf_op | source)
XLA Modules:
  0.0 49.6 jit_solution(1348655217283612068)
XLA Ops:
  0.0 48.9 %shard_map.37 = f32[32,2048]{1,0:T(8,128)S(1)} custom-call(bf16[2048,1024]{1,0:T(8,128)(2,1)} %train_hbm.1, bf16[16,1024]{1,0:T(8,128)(2,1)} %query_hbm.1, f32[1,1024]{1,0:T(1,128)} %bitcast.3), custom_call_target="tpu_custom_call" | custom-call | flops 2147483648 | bytes 6291456 | tf_op jit(solution)/shard_map/pallas_call | solution.py:400
  48.9 0.7 %copy.5 = f32[2048,32]{0,1:T(8,128)} copy(f32[2048,32]{0,1:T(8,128)S(1)} %bitcast.2) | data formatting | bytes 524288
